TPU v7x, 256 devices: a whole 4x4x8 slice. The times are simulated.
256 devices in a mesh: outer: 64 (over y_lo, z, x), inner: 4 (over y_hi, core).
Axes of the slice: x: 4, y: 4 (y_hi: 2, y_lo: 2; y = y_hi * 2 + y_lo), z: 8, core: 2. Of those that a mesh axis runs over, the one named last changes fastest.
Arguments:
- frames: bfloat16 [32768, 1024], P(('outer', 'inner')), may hold values from -6 to 6
- gain_attn: float32 [1024], replicated, may hold values from 0.5 to 2
- w_query: bfloat16 [1024, 512], replicated, may hold values from -4 to 4
- w_key: bfloat16 [1024, 512], replicated, may hold values from -0.1875 to 0.1875
- w_value: bfloat16 [1024, 512], replicated, may hold values from -0.1875 to 0.1875
- w_out: bfloat16 [512, 1024], replicated, may hold values from -0.25 to 0.25
- gain_conv: float32 [1024], replicated, may hold values from 0.5 to 2
- w_expand: bfloat16 [1024, 2048], replicated, may hold values from -0.1875 to 0.1875
- kernel_taps: float32 [31, 1024], replicated, may hold values from -2 to 2
- bn_scale: float32 [1024], replicated, may hold values from 0.5 to 2
- bn_shift: float32 [1024], replicated, may hold values from -3 to 3
- w_project: bfloat16 [1024, 1024], replicated, may hold values from -0.1875 to 0.1875
Outputs:
- block_out: bfloat16 [32768, 1024], P(('outer', 'inner'))
All inputs are finite; a program needn't handle non-finite values.
Results may differ from a plain program's by a relative error of at most 0.017.
The roundings to bfloat16 on the way count: a program that leaves them out, or rounds other values in their place, can miss the bound.
Values may be sent and summed in bfloat16 or wider, within the bound.
No kernel may reach another device: no remote copies, remote signals or barrier semaphores. Data moves between devices by JAX's collectives and lax.ppermute only.
A program may use at most 128 MiB of HBM per device.

v0:
```python
import jax
import jax.numpy as jnp
from jax import lax
from jax.sharding import PartitionSpec as P

HEAD_DIM = 64


def with_halo(cells, sides, width):
    for axis, dim in sides:
        count = lax.axis_size(axis)
        ends = count - 1
        head = lax.slice_in_dim(cells, 0, width, axis=dim)
        tail = lax.slice_in_dim(cells, cells.shape[dim] - width, cells.shape[dim], axis=dim)
        cells = jnp.concatenate(
            [
                lax.ppermute(tail, axis, [(i, (i + 1) % count) for i in range(ends)]),
                cells,
                lax.ppermute(head, axis, [((i + 1) % count, i) for i in range(ends)]),
            ],
            axis=dim,
        )
    return cells


def norm_rows(values, gain):
    values = values.astype(jnp.float32)
    center = values - jnp.mean(values, axis=-1, keepdims=True)
    spread = jnp.mean(center * center, axis=-1, keepdims=True)
    return center * lax.rsqrt(spread + 1e-05) * gain


def attend_update(carry, query_heads, key_piece, value_piece, scale):
    rows = key_piece.shape[0]
    head_count = query_heads.shape[1]
    head_size = query_heads.shape[2]
    block = 512
    key_blocks = key_piece.reshape(rows // block, block, head_count, head_size)
    value_blocks = value_piece.reshape(rows // block, block, head_count, head_size)

    def one_block(state, pair):
        accum, top, total = state
        key_block, value_block = pair
        scores = (
            jnp.einsum("qhd,khd->qhk", query_heads, key_block, preferred_element_type=jnp.float32)
            * scale
        )
        new_top = jnp.maximum(top, jnp.max(scores, axis=-1))
        factor = jnp.exp(top - new_top)
        weights = jnp.exp(scores - new_top[:, :, None])
        total = total * factor + jnp.sum(weights, axis=-1)
        mixed = jnp.einsum(
            "qhk,khd->qhd",
            weights.astype(jnp.bfloat16),
            value_block,
            preferred_element_type=jnp.float32,
        )
        accum = accum * factor[:, :, None] + mixed
        return ((accum, new_top, total), None)

    carry, unused = lax.scan(one_block, carry, (key_blocks, value_blocks))
    return carry


def body(
    frames,
    gain_attn,
    w_query,
    w_key,
    w_value,
    w_out,
    gain_conv,
    w_expand,
    kernel_taps,
    bn_scale,
    bn_shift,
    w_project,
):
    own_rows = frames.shape[0]
    model_width = frames.shape[1]
    group = lax.axis_size("inner")
    head_size = HEAD_DIM
    width = w_query.shape[1]
    local_width = width // group
    local_heads = local_width // head_size
    scale = head_size ** (-0.5)
    normed = norm_rows(frames, gain_attn).astype(jnp.bfloat16)
    start_col = lax.axis_index("inner") * local_width
    chosen = jnp.concatenate(
        [
            lax.dynamic_slice_in_dim(w_query, start_col, local_width, 1),
            lax.dynamic_slice_in_dim(w_key, start_col, local_width, 1),
            lax.dynamic_slice_in_dim(w_value, start_col, local_width, 1),
        ],
        axis=1,
    )
    projected = jnp.dot(
        lax.all_gather(normed, "inner", axis=0, tiled=True),
        chosen,
        preferred_element_type=jnp.float32,
    ).astype(jnp.bfloat16)
    query_local = projected[:, :local_width]
    key_local = projected[:, local_width : 2 * local_width]
    value_local = projected[:, 2 * local_width :]
    block_rows = group * own_rows
    query_heads = query_local.reshape(block_rows, local_heads, head_size)
    start_state = (
        jnp.zeros((block_rows, local_heads, head_size), jnp.float32),
        jnp.full((block_rows, local_heads), -jnp.inf, jnp.float32),
        jnp.zeros((block_rows, local_heads), jnp.float32),
    )
    final_state = attend_update(
        start_state,
        query_heads,
        lax.all_gather(key_local, "outer", axis=0, tiled=True),
        lax.all_gather(value_local, "outer", axis=0, tiled=True),
        scale,
    )
    accum, top, total = final_state
    context_local = (
        (accum / total[:, :, None]).astype(jnp.bfloat16).reshape(block_rows, 1, local_width)
    )
    returned = lax.all_to_all(context_local, "inner", split_axis=0, concat_axis=1, tiled=True)
    context = returned.reshape(own_rows, width)
    attn = jnp.dot(context, w_out, preferred_element_type=jnp.float32)
    hidden = (frames.astype(jnp.float32) + attn).astype(jnp.bfloat16)
    normed2 = norm_rows(hidden, gain_conv).astype(jnp.bfloat16)
    expand = jnp.dot(normed2, w_expand, preferred_element_type=jnp.float32)
    glu = (expand[:, :model_width] * jax.nn.sigmoid(expand[:, model_width:])).astype(jnp.bfloat16)
    taps = kernel_taps.shape[0]
    half_kernel = taps // 2
    padded = with_halo(glu, ((("outer", "inner"), 0),), half_kernel)
    conv = jnp.zeros((own_rows, model_width), jnp.float32)
    for tap in range(taps):
        conv = conv + kernel_taps[tap] * padded[tap : tap + own_rows].astype(jnp.float32)
    act = jax.nn.silu(bn_scale * conv + bn_shift).astype(jnp.bfloat16)
    result = hidden.astype(jnp.float32) + jnp.dot(
        act, w_project, preferred_element_type=jnp.float32
    )
    return result.astype(jnp.bfloat16)


def solution(mesh):
    return jax.shard_map(
        body,
        mesh=mesh,
        in_specs=(
            P(("outer", "inner"), None),
            P(),
            P(),
            P(),
            P(),
            P(),
            P(),
            P(),
            P(),
            P(),
            P(),
            P(),
        ),
        out_specs=P(("outer", "inner"), None),
        check_vma=False,
    )
```

profile of v0, /device:TPU:1, one launch (start us, length us, event | category | flops | bytes accessed | tf_op | source)
XLA Modules:
  0.0 1131.6 jit_solution(17595431488501985609)
XLA Ops:
  13.0 25.6 %all-gather.4.cloned.1.call-done = bf16[512,1024]{1,0:T(8,128)(2,1)} async-done(((bf16[128,1024]{1,0:T(8,128)(2,1)}), bf16[512,1024]{1,0:T(8,128)(2,1)}) %all-gather.4.cloned.1.call-update) | async-done | bytes 1048592 | tf_op jit(solution)/shard_map/all_gather | solution.py:98
  41.9 269.5 %all-gather.6.cloned.1.call-done = bf16[32768,128]{0,1:T(8,128)(2,1)} async-done(((bf16[512,128]{0,1:T(8,128)(2,1)}), bf16[32768,128]{0,1:T(8,128)(2,1)}) %all-gather.6.cloned.1.call-update) | async-done | bytes 8388624 | tf_op jit(solution)/shard_map/all_gather | solution.py:115
  311.4 10.1 copy.36
  321.6 11.3 %copy.30 = bf16[64,512,2,64]{1,3,2,0:T(8,128)(2,1)} copy(bf16[64,512,2,64]{1,0,3,2:T(8,128)(2,1)} %bitcast.89) | data formatting | bytes 16777216
  332.9 289.6 %all-gather.8.cloned.1.call-done = bf16[32768,128]{0,1:T(8,128)(2,1)} async-done(((bf16[512,128]{0,1:T(8,128)(2,1)}), bf16[32768,128]{0,1:T(8,128)(2,1)}) %all-gather.8.cloned.1.call-update) | async-done | bytes 8388624 | tf_op jit(solution)/shard_map/all_gather | solution.py:116
  622.5 10.3 copy.37
  632.8 11.4 %copy.31 = bf16[64,512,2,64]{1,3,2,0:T(8,128)(2,1)} copy(bf16[64,512,2,64]{1,0,3,2:T(8,128)(2,1)} %bitcast.90) | data formatting | bytes 16777216
  644.2 409.9 %while.15 = (s32[]{:T(128)}, f32[512,2,64]{0,2,1:T(8,128)S(1)}, f32[512,2]{0,1:T(2,128)S(1)}, f32[512,2]{0,1:T(2,128)S(1)}, bf16[64,512,2,64]{1,3,2,0:T(8,128)(2...) while((s32[]{:T(128)}, f32[512,2,64]{0,2,1:T(8,128)S(1)}, ...), condition=%wide.region_5.6_spmd.clone, body=%wide.region_2.5_spmd.clone.sunk | while | flops 138613760 | bytes 15664261 | solution.py:61
  644.2 2.8 bitcast_reduce_fusion.2
  650.6 2.7 bitcast_reduce_fusion.2
  663.4 2.7 bitcast_reduce_fusion.2
  676.2 2.7 bitcast_reduce_fusion.2
  689.0 2.7 bitcast_reduce_fusion.2
  701.9 2.7 bitcast_reduce_fusion.2
  714.7 2.7 bitcast_reduce_fusion.2
  727.5 2.7 bitcast_reduce_fusion.2
  740.3 2.7 bitcast_reduce_fusion.2
  881.2 2.7 bitcast_reduce_fusion.2
  1056.1 45.4 %all-to-all-start = ((bf16[4,2,8192]{2,1,0:T(2,128)(2,1)}), bf16[4,2,8192]{2,1,0:T(2,128)(2,1)S(1)}, u32[]{:S(2)}, u32[]{:S(2)}) async-start(bf16[4,2,8192]{2,1,0:T(2,128)(2,1)} %reshape.52), calls=%async_computation | async-start | bytes 262144 | tf_op jit(solution)/shard_map/all_to_all | solution.py:123
  1101.6 5.0 all-to-all-done
  1108.9 3.0 fusion.35
  1112.0 2.9 collective-permute-start
  1116.9 4.8 collective-permute-done.1
  1121.7 3.4 fusion.19
  (550 shorter events, 396.2 us)
Async XLA Ops:
  6.5 1115.1 %copy-start = (bf16[1024,1024]{1,0:T(8,128)(2,1)S(1)}, bf16[1024,1024]{1,0:T(8,128)(2,1)}, u32[]{:S(2)}) copy-start(bf16[1024,1024]{1,0:T(8,128)(2,1)} %param.25) | copy-start | bytes 6291460
  6.5 32.0 %all-gather.4.cloned.1.call-start = ((), (), s32[]{:S(2)}) async-start(), calls=%async_computation.1 | async-start | bytes 1310720 | tf_op jit(solution)/shard_map/all_gather | solution.py:98
  10.9 300.6 %all-gather.6.cloned.1.call-start = ((), (), s32[]{:S(2)}) async-start(), calls=%async_computation.2 | async-start | bytes 8519680 | tf_op jit(solution)/shard_map/all_gather | solution.py:115
  41.1 581.4 %all-gather.8.cloned.1.call-start = ((), (), s32[]{:S(2)}) async-start(), calls=%async_computation.3 | async-start | bytes 8519680 | tf_op jit(solution)/shard_map/all_gather | solution.py:116
  644.2 457.4 %copy-start.3 = (f32[31,1024]{1,0:T(8,128)S(1)}, f32[31,1024]{1,0:T(8,128)}, u32[]{:S(2)}) copy-start(f32[31,1024]{1,0:T(8,128)} %param.22) | copy-start | bytes 380932
  647.0 2.2 copy-start.1
  653.4 2.2 copy-start.1
  659.8 2.2 copy-start.1
  666.2 2.2 copy-start.1
  672.6 2.2 copy-start.1
  679.0 2.2 copy-start.1
  685.4 2.2 copy-start.1
  691.8 2.2 copy-start.1
  698.2 2.2 copy-start.1
  704.6 2.2 copy-start.1
  711.0 2.2 copy-start.1
  717.4 2.2 copy-start.1
  1054.1 52.9 %copy-start.2 = (bf16[128,1024]{1,0:T(8,128)(2,1)S(1)}, bf16[128,1024]{1,0:T(8,128)(2,1)}, u32[]{:S(2)}) copy-start(bf16[128,1024]{1,0:T(8,128)(2,1)} %param.14) | copy-start | bytes 786436
  1055.4 53.4 %copy-start.4 = (f32[1024]{0:T(1024)S(1)}, f32[1024]{0:T(1024)}, u32[]{:S(2)}) copy-start(f32[1024]{0:T(1024)} %param.20) | copy-start | bytes 12292
  1056.1 50.5 %all-to-all-start = ((bf16[4,2,8192]{2,1,0:T(2,128)(2,1)}), bf16[4,2,8192]{2,1,0:T(2,128)(2,1)S(1)}, u32[]{:S(2)}, u32[]{:S(2)}) async-start(bf16[4,2,8192]{2,1,0:T(2,128)(2,1)} %reshape.52), calls=%async_computation | async-start | bytes 262144 | tf_op jit(solution)/shard_map/all_to_all | solution.py:123
  1108.8 12.8 %copy-start.5 = (f32[1024]{0:T(1024)S(1)}, f32[1024]{0:T(1024)}, u32[]{:S(2)}) copy-start(f32[1024]{0:T(1024)} %param.24) | copy-start | bytes 12292
  1108.9 12.8 %copy-start.6 = (f32[1024]{0:T(1024)S(1)}, f32[1024]{0:T(1024)}, u32[]{:S(2)}) copy-start(f32[1024]{0:T(1024)} %param.23) | copy-start | bytes 12292
  1112.0 4.9 collective-permute-start
  1114.9 6.7 collective-permute-start.1
  (52 other events, 115.5 us)
Sparse Core Ops, SparseCore 0:
  11.0 27.5 all-gather.3
  41.3 270.1 all-gather.5
  313.2 309.2 all-gather.7
where the time goes:
time: 1130 us
  waiting for transfers between devices  595 us (53%)
  matrix products  275 us (24%)
  other arithmetic  141 us (12%)
  local copies, waits for them, and re-layouts  53.5 us (5%)
  starting transfers between devices  50.3 us (4%)
  between operations  13.3 us (1%)
    all_gather x1, waiting for transfers between devices, body(): lax.all_gather(value_local, 'outer', axis=0, tiled=True)  290 us
    all_gather x1, waiting for transfers between devices, body(): lax.all_gather(key_local, 'outer', axis=0, tiled=True)  270 us
    dot_general x64, matrix products, one_block(): jnp.einsum('qhd,khd->qhk', query_heads, key_block, preferred_element_type...  175 us
    reduce_sum x64, other arithmetic, one_block(): total = total * factor + jnp.sum(weights, axis=-1)  134 us
    dot_general x64, matrix products, one_block(): jnp.einsum('qhk,khd->qhd', weights.astype(jnp.bfloat16), value_block, pre...  90.4 us
    all_to_all x1, starting transfers between devices, body(): lax.all_to_all(context_local, 'inner', split_axis=0, concat_axis=1, tiled...  45.4 us
    unnamed x20, local copies, waits for them, and re-layouts  44.1 us
    all_gather x1, waiting for transfers between devices, body(): lax.all_gather(normed, 'inner', axis=0, tiled=True)  25.6 us
  transfers between devices with their start and end apart: 6, of which 5 were waited for; matrix products, arithmetic and copies ran while one was open for 2% of the time, Pallas kernels for 0%

commit v1 on v0

--- a/solution.py
+++ b/solution.py
@@ -112,7 +112,9 @@
     final_state = attend_update(
         start_state,
         query_heads,
-        lax.all_gather(key_local, "outer", axis=0, tiled=True),
+        jnp.concatenate(
+            lax.all_to_all(jnp.stack([key_local] * lax.axis_size("outer")), "outer", 0, 0), axis=0
+        ),
         lax.all_gather(value_local, "outer", axis=0, tiled=True),
         scale,
     )

time: 1130 us -> 904 us (0.80)
  waiting for transfers between devices: 595 us -> 383 us
  local copies, waits for them, and re-layouts: 53.5 us -> 36.1 us
    all_gather x1 -> x0, waiting for transfers between devices: 270 us -> none  [body(): lax.all_gather(key_local, 'outer', axis=0, tiled=True)]
    all_gather x1, waiting for transfers between devices: 290 us -> 347 us  [body(): lax.all_gather(value_local, 'outer', axis=0, tiled=True)]
    unnamed x20 -> x18, local copies, waits for them, and re-layouts: 44.1 us -> 22.5 us
    all_to_all x1, starting transfers between devices: 45.4 us -> 33.6 us  [body(): lax.all_to_all(context_local, 'inner', split_axis=0, concat_axis=1, tiled...]
  transfers between devices with their start and end apart: 6 -> 6, of which waited for: 5 -> 4; matrix products, arithmetic and copies ran while one was open for 2% -> 3% of each run, Pallas kernels for 0% -> 0%
where the time goes in v1:
time: 904 us; the launch traced here: 901 us
  waiting for transfers between devices  383 us (42%)
  matrix products  276 us (31%)
  other arithmetic  141 us (16%)
  starting transfers between devices  49.3 us (5%)
  local copies, waits for them, and re-layouts  36.1 us (4%)
  between operations  13.6 us (2%)
    all_gather x1, waiting for transfers between devices, body(): lax.all_gather(value_local, 'outer', axis=0, tiled=True)  347 us
    dot_general x64, matrix products, one_block(): jnp.einsum('qhd,khd->qhk', query_heads, key_block, preferred_element_type...  175 us
    reduce_sum x64, other arithmetic, one_block(): total = total * factor + jnp.sum(weights, axis=-1)  134 us
    dot_general x64, matrix products, one_block(): jnp.einsum('qhk,khd->qhd', weights.astype(jnp.bfloat16), value_block, pre...  90.4 us
    all_to_all x1, starting transfers between devices, body(): lax.all_to_all(context_local, 'inner', split_axis=0, concat_axis=1, tiled...  33.6 us
    all_gather x1, waiting for transfers between devices, body(): lax.all_gather(normed, 'inner', axis=0, tiled=True)  25.6 us
    unnamed x18, local copies, waits for them, and re-layouts  22.5 us
  transfers between devices with their start and end apart: 6, of which 4 were waited for; matrix products, arithmetic and copies ran while one was open for 3% of the time, Pallas kernels for 0%

profile of v1, /device:TPU:1, one launch (start us, length us, event | category | flops | bytes accessed | tf_op | source)
XLA Modules:
  0.0 901.2 jit_solution(15976897597471925591)
XLA Ops:
  13.0 25.6 %all-gather.3.cloned.1.call-done = bf16[512,1024]{1,0:T(8,128)(2,1)} async-done(((bf16[128,1024]{1,0:T(8,128)(2,1)}), bf16[512,1024]{1,0:T(8,128)(2,1)}) %all-gather.3.cloned.1.call-update) | async-done | bytes 1048592 | tf_op jit(solution)/shard_map/all_gather | solution.py:98
  41.1 4.2 stack.2
  45.4 10.6 %all-to-all-start = ((bf16[64,512,128]{1,2,0:T(8,128)(2,1)}), bf16[64,512,128]{1,2,0:T(8,128)(2,1)}, u32[]{:S(2)}, u32[]{:S(2)}) async-start(bf16[64,512,128]{1,2,0:T(8,128)(2,1)} %stack.2), calls=%async_computation | async-start | bytes 16777216 | tf_op jit(solution)/shard_map/all_to_all | solution.py:116
  56.0 347.5 %all-gather.5.cloned.1.call-done = bf16[32768,128]{0,1:T(8,128)(2,1)} async-done(((bf16[512,128]{0,1:T(8,128)(2,1)}), bf16[32768,128]{0,1:T(8,128)(2,1)}) %all-gather.5.cloned.1.call-update) | async-done | bytes 8388624 | tf_op jit(solution)/shard_map/all_gather | solution.py:118
  403.5 10.1 %copy.31 = bf16[16,8,64,512]{3,2,1,0:T(8,128)(2,1)} copy(bf16[16,8,64,512]{3,1,2,0:T(8,128)(2,1)} %bitcast.86) | data formatting | bytes 16777216
  413.6 11.3 %copy.26 = bf16[64,512,2,64]{1,3,2,0:T(8,128)(2,1)} copy(bf16[64,512,2,64]{1,0,3,2:T(8,128)(2,1)} %bitcast.85) | data formatting | bytes 16777216
  425.0 410.2 %while.15 = (s32[]{:T(128)}, f32[512,2,64]{0,2,1:T(8,128)S(1)}, f32[512,2]{0,1:T(2,128)S(1)}, f32[512,2]{0,1:T(2,128)S(1)}, bf16[64,512,2,64]{1,3,2,0:T(8,128)(2...) while((s32[]{:T(128)}, f32[512,2,64]{0,2,1:T(8,128)S(1)}, ...), condition=%wide.region_5.6_spmd.clone, body=%wide.region_2.5_spmd.clone.sunk | while | flops 138613760 | bytes 15664261 | solution.py:61
  425.0 2.8 bitcast_reduce_fusion.2
  437.8 2.7 bitcast_reduce_fusion.2
  444.2 2.7 bitcast_reduce_fusion.2
  501.9 2.7 bitcast_reduce_fusion.2
  540.4 2.7 bitcast_reduce_fusion.2
  546.8 2.7 bitcast_reduce_fusion.2
  604.5 2.7 bitcast_reduce_fusion.2
  642.9 2.7 bitcast_reduce_fusion.2
  649.3 2.7 bitcast_reduce_fusion.2
  694.2 2.7 bitcast_reduce_fusion.2
  700.6 2.7 bitcast_reduce_fusion.2
  837.3 33.6 %all-to-all-start.1 = ((bf16[4,2,8192]{2,1,0:T(2,128)(2,1)}), bf16[4,2,8192]{2,1,0:T(2,128)(2,1)S(1)}, u32[]{:S(2)}, u32[]{:S(2)}) async-start(bf16[4,2,8192]{2,1,0:T(2,128)(2,1)} %reshape.50), calls=%async_computation.1 | async-start | bytes 262144 | tf_op jit(solution)/shard_map/all_to_all | solution.py:125
  870.9 5.0 all-to-all-done.1
  878.2 3.0 fusion.35
  881.3 2.9 collective-permute-start
  886.5 4.5 collective-permute-done.1
  891.0 3.4 fusion.19
  (548 shorter events, 393.2 us)
Async XLA Ops:
  6.5 884.5 %copy-start = (bf16[1024,1024]{1,0:T(8,128)(2,1)S(1)}, bf16[1024,1024]{1,0:T(8,128)(2,1)}, u32[]{:S(2)}) copy-start(bf16[1024,1024]{1,0:T(8,128)(2,1)} %param.25) | copy-start | bytes 6291460
  6.5 32.0 %all-gather.3.cloned.1.call-start = ((), (), s32[]{:S(2)}) async-start(), calls=%async_computation.2 | async-start | bytes 1310720 | tf_op jit(solution)/shard_map/all_gather | solution.py:98
  10.9 392.6 %all-gather.5.cloned.1.call-start = ((), (), s32[]{:S(2)}) async-start(), calls=%async_computation.3 | async-start | bytes 8519680 | tf_op jit(solution)/shard_map/all_gather | solution.py:118
  45.4 379.6 %all-to-all-start = ((bf16[64,512,128]{1,2,0:T(8,128)(2,1)}), bf16[64,512,128]{1,2,0:T(8,128)(2,1)}, u32[]{:S(2)}, u32[]{:S(2)}) async-start(bf16[64,512,128]{1,2,0:T(8,128)(2,1)} %stack.2), calls=%async_computation | async-start | bytes 16777216 | tf_op jit(solution)/shard_map/all_to_all | solution.py:116
  425.0 445.9 %copy-start.3 = (f32[31,1024]{1,0:T(8,128)S(1)}, f32[31,1024]{1,0:T(8,128)}, u32[]{:S(2)}) copy-start(f32[31,1024]{1,0:T(8,128)} %param.22) | copy-start | bytes 380932
  427.7 2.2 copy-start.1
  434.2 2.2 copy-start.1
  440.6 2.2 copy-start.1
  447.0 2.2 copy-start.1
  453.4 2.2 copy-start.1
  459.8 2.2 copy-start.1
  466.2 2.2 copy-start.1
  472.6 2.2 copy-start.1
  485.4 2.2 copy-start.1
  504.7 2.2 copy-start.1
  511.1 2.2 copy-start.1
  517.5 2.2 copy-start.1
  835.2 41.1 %copy-start.2 = (bf16[128,1024]{1,0:T(8,128)(2,1)S(1)}, bf16[128,1024]{1,0:T(8,128)(2,1)}, u32[]{:S(2)}) copy-start(bf16[128,1024]{1,0:T(8,128)(2,1)} %param.14) | copy-start | bytes 786436
  836.6 41.6 %copy-start.4 = (f32[1024]{0:T(1024)S(1)}, f32[1024]{0:T(1024)}, u32[]{:S(2)}) copy-start(f32[1024]{0:T(1024)} %param.20) | copy-start | bytes 12292
  837.3 38.7 %all-to-all-start.1 = ((bf16[4,2,8192]{2,1,0:T(2,128)(2,1)}), bf16[4,2,8192]{2,1,0:T(2,128)(2,1)S(1)}, u32[]{:S(2)}, u32[]{:S(2)}) async-start(bf16[4,2,8192]{2,1,0:T(2,128)(2,1)} %reshape.50), calls=%async_computation.1 | async-start | bytes 262144 | tf_op jit(solution)/shard_map/all_to_all | solution.py:125
  878.1 12.8 %copy-start.5 = (f32[1024]{0:T(1024)S(1)}, f32[1024]{0:T(1024)}, u32[]{:S(2)}) copy-start(f32[1024]{0:T(1024)} %param.24) | copy-start | bytes 12292
  878.2 12.8 %copy-start.6 = (f32[1024]{0:T(1024)S(1)}, f32[1024]{0:T(1024)}, u32[]{:S(2)}) copy-start(f32[1024]{0:T(1024)} %param.23) | copy-start | bytes 12292
  881.3 5.1 collective-permute-start
  884.2 6.7 collective-permute-start.1
  (52 other events, 115.5 us)
Sparse Core Ops, SparseCore 0:
  11.0 27.5 all-gather.2
  41.2 362.2 all-gather.4
